TPU v7x, 1024 devices: a whole 8x8x8 slice. The times are simulated.
1024 devices in a mesh: samp: 8 (over x), proto: 128 (over y, z, core).
Axes of the slice: x: 8, y: 8, z: 8, core: 2. Of those that a mesh axis runs over, the one named last changes fastest.
Arguments:
- embeddings: bfloat16 [2, 4096, 256], P(None, 'samp'), may hold values from -60 to 60
- prototypes: bfloat16 [65536, 256], P('proto'), may hold values from -12 to 12
Outputs:
- grad_embed: bfloat16 [2, 4096, 256], P(None, 'samp')
- grad_proto: bfloat16 [65536, 256], P('proto')
- loss: float32 [2, 4096], P(None, 'samp')
All inputs are finite; a program needn't handle non-finite values.
Results may differ from a plain program's by a relative error of at most 0.001.
The roundings to bfloat16 on the way count: a program that leaves them out, or rounds other values in their place, can miss the bound.
Values may be sent and summed in bfloat16 or wider, within the bound.
A program may use at most 32 MiB of HBM per device.

v0:
```python
import jax
import jax.numpy as jnp
from jax import lax
from jax.sharding import PartitionSpec as P

ITERS = 3


EPS_SINK = 0.05
TEMPER = 0.1


def normalize_rows(values):
    as_float = values.astype(jnp.float32)
    inverse = lax.rsqrt(jnp.sum(as_float * as_float, axis=-1, keepdims=True) + 1e-06)
    return (as_float * inverse, inverse)


def project(summed, unit_rows, inverse):
    return (summed - unit_rows * jnp.sum(unit_rows * summed, axis=-1, keepdims=True)) * inverse


def body(embeddings, prototypes):
    per_view = embeddings.shape[1]
    unit_emb, inverse_emb = normalize_rows(embeddings)
    unit_proto, inverse_proto = normalize_rows(prototypes)
    emb_b = unit_emb.astype(jnp.bfloat16)
    proto_b = unit_proto.astype(jnp.bfloat16)
    scores = jnp.einsum("vbd,kd->vbk", emb_b, proto_b, preferred_element_type=jnp.float32)
    sink_exp = jnp.exp(scores / EPS_SINK)
    soft_exp = jnp.exp(scores / TEMPER)
    weights = jnp.ones((2, per_view), jnp.float32)
    proto_scale = jnp.ones((2, scores.shape[2]), jnp.float32)
    soft_total = weights
    cross_total = weights
    for sweep in range(ITERS):
        column_sums = jnp.sum(sink_exp * weights[:, :, None], axis=1)
        proto_scale = 1.0 / lax.psum(column_sums, "samp")
        row_sums = jnp.sum(sink_exp * proto_scale[:, None, :], axis=2)
        extras = []
        if sweep == 0:
            extras.append(jnp.sum(soft_exp, axis=2))
        if sweep == ITERS - 1:
            scaled_swap = (sink_exp * proto_scale[:, None, :])[::-1]
            extras.append(jnp.sum(scaled_swap * scores, axis=2))
        totals = lax.psum(jnp.stack([row_sums] + extras), "proto")
        weights = 1.0 / totals[0]
        if sweep == 0:
            soft_total = totals[1]
        if sweep == ITERS - 1:
            cross_total = totals[len(extras)]
    loss = jnp.log(soft_total) - cross_total * weights[::-1] / TEMPER
    assign = sink_exp * proto_scale[:, None, :] * weights[:, :, None]
    softmax_p = soft_exp / soft_total[:, :, None]
    slope_bf = ((softmax_p - assign[::-1]) / TEMPER).astype(jnp.bfloat16)
    proto_part = jnp.einsum("vbk,vbd->kd", slope_bf, emb_b, preferred_element_type=jnp.float32)
    proto_grad = lax.psum(proto_part, "samp")
    grad_proto = project(proto_grad, unit_proto, inverse_proto).astype(jnp.bfloat16)
    emb_part = jnp.einsum("vbk,kd->vbd", slope_bf, proto_b, preferred_element_type=jnp.float32)
    emb_grad = lax.psum(emb_part, "proto")
    grad_embed = project(emb_grad, unit_emb, inverse_emb).astype(jnp.bfloat16)
    return (grad_embed, grad_proto, loss)


def solution(mesh):
    return jax.shard_map(
        body,
        mesh=mesh,
        in_specs=(P(None, "samp", None), P("proto", None)),
        out_specs=(P(None, "samp", None), P("proto", None), P(None, "samp")),
        check_vma=False,
    )
```

profile of v0, /device:TPU:1, one launch (start us, length us, event | category | flops | bytes accessed | tf_op | source)
XLA Modules:
  0.0 1118.8 jit_solution(18409499534772170617)
XLA Ops:
  7.2 0.0 all-reduce.3.cloned.1.call-start
  7.2 1.1 fusion.21
  8.3 1.3 fusion.12
  9.6 1.8 fusion.13
  11.4 14.1 %psum.56 = f32[2,512]{1,0:T(2,128)S(1)} all-reduce(f32[2,512]{1,0:T(2,128)S(1)} %get-tuple-element.11), channel_id=1, replica_groups=mesh['samp'=8,'proto'=128] {'samp'}, use_global_device_ids=true, to_apply=%region_3.0 | all-reduce | flops 1024 | bytes 8192 | tf_op jit(solution)/shard_map/psum | solution.py:38
  25.5 0.7 multiply_reduce_fusion.4
  26.2 268.8 %psum.57 = f32[2,2,512]{2,1,0:T(2,128)S(1)} all-reduce(f32[2,2,512]{2,1,0:T(2,128)S(1)} %pad_maximum_fusion), channel_id=1, replica_groups=mesh['samp'=8,'proto'=128] {'proto'}, use_global_device_ids=true, to_apply=%region_6.0 | all-reduce | flops 2048 | bytes 16384 | tf_op jit(solution)/shard_map/psum | solution.py:46
  295.0 0.4 multiply_reduce_fusion.3
  295.4 11.8 %psum.58 = f32[2,512]{1,0:T(2,128)S(1)} all-reduce(f32[2,512]{1,0:T(2,128)S(1)} %multiply_reduce_fusion.3), channel_id=1, replica_groups=mesh['samp'=8,'proto'=128] {'samp'}, use_global_device_ids=true, to_apply=%region_8.0 | all-reduce | flops 1024 | bytes 8192 | tf_op jit(solution)/shard_map/psum | solution.py:38
  307.2 0.4 multiply_reduce_fusion.2
  307.6 251.1 %psum.59 = f32[1,2,512]{2,1,0:T(2,128)S(1)} all-reduce(f32[1,2,512]{2,1,0:T(2,128)S(1)} %bitcast.33), channel_id=1, replica_groups=mesh['samp'=8,'proto'=128] {'proto'}, use_global_device_ids=true, to_apply=%region_10.0 | all-reduce | flops 1024 | bytes 8192 | tf_op jit(solution)/shard_map/psum | solution.py:46
  558.7 0.4 multiply_reduce_fusion.1
  559.1 11.2 %psum.60 = f32[2,512]{1,0:T(2,128)S(1)} all-reduce(f32[2,512]{1,0:T(2,128)S(1)} %multiply_reduce_fusion.1), channel_id=1, replica_groups=mesh['samp'=8,'proto'=128] {'samp'}, use_global_device_ids=true, to_apply=%region_12.0 | all-reduce | flops 1024 | bytes 8192 | tf_op jit(solution)/shard_map/psum | solution.py:38
  570.3 0.3 broadcast_multiply_fusion.1
  570.7 0.6 fusion.31
  571.3 254.6 %psum.61 = f32[2,2,512]{2,1,0:T(2,128)S(1)} all-reduce(f32[2,2,512]{2,1,0:T(2,128)S(1)} %pad_maximum_fusion.1), channel_id=1, replica_groups=mesh['samp'=8,'proto'=128] {'proto'}, use_global_device_ids=true, to_apply=%region_15.0 | all-reduce | flops 2048 | bytes 16384 | tf_op jit(solution)/shard_map/psum | solution.py:46
  825.9 0.1 reverse.3
  826.1 0.6 multiply_subtract_fusion
  826.7 0.4 broadcast_multiply_fusion
  827.1 0.0 copy-start
  827.1 0.6 multiply_convert_fusion
  827.6 0.4 copy-done
  828.0 0.0 copy-start.1
  828.0 1.6 fusion.27
  829.6 0.0 all-reduce.3.cloned.1.call-update
  829.6 0.0 all-reduce.5.cloned.1.call-start
  829.7 0.0 copy-done.1
  829.7 1.4 convolution_bitcast_fusion
  831.1 0.0 all-reduce.5.cloned.1.call-update
  831.1 197.3 %all-reduce.3.cloned.1.call-done = f32[2,512,256]{2,1,0:T(8,128)} async-done(((f32[2,512,256]{2,1,0:T(8,128)}), f32[2,512,256]{2,1,0:T(8,128)}) %all-reduce.3.cloned.1.call-update) | async-done | bytes 1048592 | tf_op jit(solution)/shard_map/psum | solution.py:60
  1028.4 7.6 fusion.9
  1036.0 72.8 %all-reduce.5.cloned.1.call-done = f32[512,256]{1,0:T(8,128)} async-done(((f32[512,256]{1,0:T(8,128)}), f32[512,256]{1,0:T(8,128)}) %all-reduce.5.cloned.1.call-update) | async-done | bytes 524304 | tf_op jit(solution)/shard_map/psum | solution.py:57
  1108.8 1.3 fusion.17
  1110.0 2.0 fusion.20
  (10 shorter events, 0.1 us)
Async XLA Ops:
  7.2 1021.2 %all-reduce.3.cloned.1.call-start = ((), (), s32[]{:S(2)}) async-start(), calls=%async_computation | async-start | bytes 2097152 | tf_op jit(solution)/shard_map/psum | solution.py:60
  827.1 1.0 copy-start
  828.0 1.7 copy-start.1
  829.6 279.1 %all-reduce.5.cloned.1.call-start = ((), (), s32[]{:S(2)}) async-start(), calls=%async_computation.1 | async-start | bytes 1048576 | tf_op jit(solution)/shard_map/psum | solution.py:57
Sparse Core Ops, SparseCore 0:
  829.8 198.5 all-reduce.2
  1030.7 78.0 all-reduce.4
where the time goes:
time: 1120 us
  blocking collectives  812 us (72%)
  waiting for transfers between devices  270 us (24%)
  other arithmetic  17.6 us (2%)
  between operations  14.2 us (1%)
    psum x3, blocking collectives, body(): totals = lax.psum(jnp.stack([row_sums] + extras), 'proto')  775 us
    psum x1, waiting for transfers between devices, body(): emb_grad = lax.psum(emb_part, 'proto')  197 us
    psum x1, waiting for transfers between devices, body(): proto_grad = lax.psum(proto_part, 'samp')  72.8 us
    psum x3, blocking collectives, body(): proto_scale = 1.0 / lax.psum(column_sums, 'samp')  37 us
  transfers between devices with their start and end apart: 2, of which 2 were waited for; matrix products, arithmetic and copies ran while one was open for 1% of the time, Pallas kernels for 0%

commit v1 on v0

v1 whole, which is shorter than its diff:
```python
import functools

import jax
import jax.numpy as jnp
from jax import lax
from jax.experimental import pallas as pl
from jax.experimental.pallas import tpu as pltpu
from jax.sharding import PartitionSpec as P

ITERS = 3
INV_TEMPER = 10.0
F32 = jnp.float32
BF16 = jnp.bfloat16
MESH = pl.DeviceIdType.MESH
LANES = 128


def normalize_rows(values):
    as_float = values.astype(F32)
    inverse = lax.rsqrt(jnp.sum(as_float * as_float, axis=-1, keepdims=True) + 1e-06)
    return as_float * inverse, inverse


def project(summed, unit_rows, inverse):
    return (summed - unit_rows * jnp.sum(unit_rows * summed, axis=-1, keepdims=True)) * inverse


def far_first(count):
    half = count // 2
    order = [half]
    for step in range(1, half + 1):
        for offset in (half - step, half + step):
            if 0 < offset < count and offset not in order:
                order.append(offset)
    return order


def kernel(
    nx,
    ny,
    emb_ref,
    proto_ref,
    ge_ref,
    gp_ref,
    loss_ref,
    eb_ref,
    pb_ref,
    s_ref,
    soft_ref,
    sink_ref,
    slope_ref,
    epart_ref,
    ppart_ref,
    wcol_ref,
    tcol_ref,
    col_buf,
    row_buf,
    rowz_buf,
    sib_buf,
    a_buf,
    b_buf,
    x_buf,
    send_sem,
    recv_sem,
):
    rows, width = eb_ref.shape
    half = rows // 2
    cols = pb_ref.shape[0]
    x = lax.axis_index("samp")
    p = lax.axis_index("proto")
    y = p // (2 * ny)
    z = (p // 2) % ny
    c = p % 2
    pos = y * 2 + c
    ai = y + (z - y) * c
    bi = z + (y - z) * c
    astep = 2 * ny + (2 - 2 * ny) * c
    bstep = 2 + (2 * ny - 2) * c
    ablock = rows // 2 // ny
    xblock = cols // nx

    def at_x(j):
        return (j, p)

    def at_yc(j):
        return (x, (j // 2) * (2 * ny) + z * 2 + j % 2)

    def at_z(j):
        return (x, y * (2 * ny) + j * 2 + c)

    def at_a(j):
        return (x, p + (j - ai) * astep)

    def at_b(j):
        return (x, p + (j - bi) * bstep)

    def at_ac(j):
        return (x, p + (j // 2 - ai) * astep + j % 2 - c)

    sibling = (x, p + 1 - 2 * c)

    barrier = pltpu.get_barrier_semaphore()

    def greet(device):
        pl.semaphore_signal(barrier, inc=1, device_id=device, device_id_type=MESH)

    for d in range(1, nx):
        greet(at_x(lax.rem(x + d, nx)))
    for d in range(1, ny):
        for core in range(2):
            greet((x, lax.rem(y + d, ny) * (2 * ny) + z * 2 + core))
            greet((x, y * (2 * ny) + lax.rem(z + d, ny) * 2 + core))
    greet(sibling)

    pending = []

    def flush():
        for copy in pending:
            copy.wait_send()
        pending.clear()

    def start(stage, count, me, at, source, place):
        for d in far_first(count):
            j = lax.rem(me + d, count)
            copy = pltpu.make_async_remote_copy(
                src_ref=source(j),
                dst_ref=place(me),
                send_sem=send_sem.at[stage, d],
                recv_sem=recv_sem.at[stage, me],
                device_id=at(j),
                device_id_type=MESH,
            )
            copy.start()
            pending.append(copy)

    def wait(stage, count, me, at, place):
        for d in range(1, count):
            j = lax.rem(me + d, count)
            pltpu.make_async_remote_copy(
                src_ref=place(j),
                dst_ref=place(j),
                send_sem=send_sem.at[stage, d],
                recv_sem=recv_sem.at[stage, j],
                device_id=at(j),
                device_id_type=MESH,
            ).wait_recv()

    def total_of(ref, count):
        total = ref[0]
        for j in range(1, count):
            total = total + ref[j]
        return total

    def wide(column):
        return jnp.concatenate([column] * (cols // LANES), axis=1)

    def narrow(block):
        total = block[:, :LANES]
        for j in range(1, cols // LANES):
            total = total + block[:, j * LANES : (j + 1) * LANES]
        return jnp.sum(total.T, axis=0, keepdims=True)

    step = min(256, half)
    blocks = [(v, i) for v in range(2) for i in range(v * half, (v + 1) * half, step)]

    unit_proto, _ = normalize_rows(proto_ref[...])
    pb_ref[...] = unit_proto.astype(BF16)
    sums = [None, None]
    for v, i in blocks:
        unit, _ = normalize_rows(emb_ref[i : i + step, :])
        eb = unit.astype(BF16)
        eb_ref[i : i + step, :] = eb
        s = lax.dot_general(eb, pb_ref[...], (((1,), (1,)), ((), ())), preferred_element_type=F32)
        s_ref[i : i + step, :] = s
        soft = jnp.exp(s * INV_TEMPER)
        soft_ref[i : i + step, :] = soft
        sink = soft * soft
        sink_ref[i : i + step, :] = sink
        part = jnp.sum(sink, axis=0, keepdims=True)
        sums[v] = part if sums[v] is None else sums[v] + part

    def store_columns(ref, row):
        for i in range(0, rows, step):
            ref[i : i + step, :] = jnp.broadcast_to(row[:, i : i + step], (LANES, step)).T

    pl.semaphore_wait(barrier, nx - 1 + 4 * (ny - 1) + 1)

    soft_total = None
    weights = None
    scale = None
    SOFT_YC, SOFT_Z = 3, 3
    for sweep in range(ITERS):
        if sweep > 0:
            sums = [None, None]
            for v, i in blocks:
                part = jnp.sum(sink_ref[i : i + step, :] * wide(wcol_ref[i : i + step, :]), axis=0, keepdims=True)
                sums[v] = part if sums[v] is None else sums[v] + part
        stage = 3 * sweep
        col = col_buf.at[sweep]
        for v in range(2):
            col[x, v : v + 1, :] = sums[v]
        start(stage, nx, x, at_x, lambda j: col.at[x], lambda j: col.at[j])
        if sweep == 0:
            for v, i in blocks:
                row_buf[SOFT_YC, pos, :, i : i + step] = narrow(soft_ref[i : i + step, :])
            extra = row_buf.at[SOFT_YC]
            start(9, 2 * ny, pos, at_yc, lambda j: extra.at[pos], lambda j: extra.at[j])
        wait(stage, nx, x, at_x, lambda j: col.at[j])
        scale = 1.0 / total_of(col, nx)
        row = row_buf.at[sweep]
        for v, i in blocks:
            row[pos, :, i : i + step] = narrow(sink_ref[i : i + step, :] * scale[v : v + 1, :])
        start(stage + 1, 2 * ny, pos, at_yc, lambda j: row.at[pos], lambda j: row.at[j])
        if sweep == 0:
            wait(9, 2 * ny, pos, at_yc, lambda j: extra.at[j])
            extraz = rowz_buf.at[SOFT_Z]
            extraz[z] = total_of(extra, 2 * ny)
            start(10, ny, z, at_z, lambda j: extraz.at[z], lambda j: extraz.at[j])
        wait(stage + 1, 2 * ny, pos, at_yc, lambda j: row.at[j])
        rowz = rowz_buf.at[sweep]
        rowz[z] = total_of(row, 2 * ny)
        start(stage + 2, ny, z, at_z, lambda j: rowz.at[z], lambda j: rowz.at[j])
        if sweep == 1:
            wait(10, ny, z, at_z, lambda j: extraz.at[j])
            soft_total = total_of(extraz, ny)
            store_columns(tcol_ref, INV_TEMPER / soft_total)
        flush()
        wait(stage + 2, ny, z, at_z, lambda j: rowz.at[j])
        weights = 1.0 / total_of(rowz, ny)
        store_columns(wcol_ref, weights)

    scaled = scale * INV_TEMPER
    for v, i in blocks:
        o = i + half * (1 - 2 * v)
        pull = sink_ref[o : o + step, :] * scaled[1 - v : 2 - v, :] * wide(wcol_ref[o : o + step, :])
        push = soft_ref[i : i + step, :] * wide(tcol_ref[i : i + step, :])
        slope = (push - pull).astype(BF16)
        slope_ref[i : i + step, :] = slope
        epart_ref[v, i - v * half : i - v * half + step, :] = jnp.dot(
            slope, pb_ref[...], preferred_element_type=F32
        )
    to_sibling = pltpu.make_async_remote_copy(
        src_ref=epart_ref.at[1 - c],
        dst_ref=sib_buf,
        send_sem=send_sem.at[11, 0],
        recv_sem=recv_sem.at[11, 0],
        device_id=sibling,
        device_id_type=MESH,
    )
    to_sibling.start()
    for k in range(0, cols, LANES):
        ppart_ref[k : k + LANES, :] = lax.dot_general(
            slope_ref[:, k : k + LANES], eb_ref[...], (((0,), (0,)), ((), ())), preferred_element_type=F32
        )
    start(12, nx, x, at_x, lambda j: ppart_ref.at[pl.ds(j * xblock, xblock)], lambda j: x_buf.at[j])
    x_buf[x] = ppart_ref[pl.ds(x * xblock, xblock), :]

    to_sibling.wait_recv()
    for i in range(0, half, step):
        sib_buf[i : i + step, :] = sib_buf[i : i + step, :] + epart_ref[c, i : i + step, :]
    start(13, ny, ai, at_a, lambda j: sib_buf.at[pl.ds(j * ablock, ablock)], lambda j: a_buf.at[j])
    a_buf[ai] = sib_buf[pl.ds(ai * ablock, ablock), :]

    CROSS_YC, CROSS_Z = 4, 4
    cross = row_buf.at[CROSS_YC]
    for v, i in blocks:
        o = i + half * (1 - 2 * v)
        cross[pos, :, i : i + step] = narrow(
            sink_ref[o : o + step, :] * scale[1 - v : 2 - v, :] * s_ref[i : i + step, :]
        )
    start(14, 2 * ny, pos, at_yc, lambda j: cross.at[pos], lambda j: cross.at[j])

    wait(13, ny, ai, at_a, lambda j: a_buf.at[j])
    b_buf[bi] = total_of(a_buf, ny)
    start(15, ny, bi, at_b, lambda j: b_buf.at[bi], lambda j: b_buf.at[j])

    wait(14, 2 * ny, pos, at_yc, lambda j: cross.at[j])
    crossz = rowz_buf.at[CROSS_Z]
    crossz[z] = total_of(cross, 2 * ny)
    start(16, ny, z, at_z, lambda j: crossz.at[z], lambda j: crossz.at[j])

    wait(12, nx, x, at_x, lambda j: x_buf.at[j])
    unit, inverse = normalize_rows(proto_ref[pl.ds(x * xblock, xblock), :])
    gp_ref[pl.ds(x * xblock, xblock), :] = project(total_of(x_buf, nx), unit, inverse).astype(BF16)
    start(
        17,
        nx,
        x,
        at_x,
        lambda j: gp_ref.at[pl.ds(x * xblock, xblock)],
        lambda j: gp_ref.at[pl.ds(j * xblock, xblock)],
    )

    base = c * half + ai * ablock
    unit, inverse = normalize_rows(emb_ref[pl.ds(base, ablock), :])
    wait(15, ny, bi, at_b, lambda j: b_buf.at[j])
    ge_ref[pl.ds(base, ablock), :] = project(total_of(b_buf, ny), unit, inverse).astype(BF16)

    def ge_place(j):
        return ge_ref.at[pl.ds((j % 2) * half + (j // 2) * ablock, ablock)]

    mine = ge_ref.at[pl.ds(base, ablock)]
    for d in far_first(ny):
        j = lax.rem(ai + d, ny)
        for other in range(2):
            copy = pltpu.make_async_remote_copy(
                src_ref=mine,
                dst_ref=mine,
                send_sem=send_sem.at[18 + other, d],
                recv_sem=recv_sem.at[18 + other, ai],
                device_id=(x, p + (j - ai) * astep + other * (1 - 2 * c)),
                device_id_type=MESH,
            )
            copy.start()
            pending.append(copy)
    across = pltpu.make_async_remote_copy(
        src_ref=mine,
        dst_ref=mine,
        send_sem=send_sem.at[19, 0],
        recv_sem=recv_sem.at[19, ai],
        device_id=sibling,
        device_id_type=MESH,
    )
    across.start()
    pending.append(across)

    wait(16, ny, z, at_z, lambda j: crossz.at[j])
    cross_total = total_of(crossz, ny)
    swapped = jnp.concatenate([weights[:, half:], weights[:, :half]], axis=1)
    loss = jnp.log(soft_total) - cross_total * swapped * INV_TEMPER
    loss_ref[0:1, :] = loss[:, :half]
    loss_ref[1:2, :] = loss[:, half:]
    to_sibling.wait_send()
    flush()
    wait(17, nx, x, at_x, lambda j: gp_ref.at[pl.ds(j * xblock, xblock)])
    for d in range(1, ny):
        j = lax.rem(ai + d, ny)
        place = ge_ref.at[pl.ds(c * half + j * ablock, ablock)]
        pltpu.make_async_remote_copy(
            src_ref=place,
            dst_ref=place,
            send_sem=send_sem.at[18, d],
            recv_sem=recv_sem.at[18, j],
            device_id=at_a(j),
            device_id_type=MESH,
        ).wait_recv()
    for j in range(ny):
        place = ge_ref.at[pl.ds((1 - c) * half + j * ablock, ablock)]
        pltpu.make_async_remote_copy(
            src_ref=place,
            dst_ref=place,
            send_sem=send_sem.at[19, 0],
            recv_sem=recv_sem.at[19, j],
            device_id=sibling,
            device_id_type=MESH,
        ).wait_recv()


def body(nx, ny, embeddings, prototypes):
    views, samples, width = embeddings.shape
    rows, cols = views * samples, prototypes.shape[0]
    ablock, xblock = samples // ny, cols // nx
    vmem = pl.BlockSpec(memory_space=pltpu.VMEM)
    ge, gp, loss = pl.pallas_call(
        functools.partial(kernel, nx, ny),
        out_shape=(
            jax.ShapeDtypeStruct((rows, width), BF16),
            jax.ShapeDtypeStruct((cols, width), BF16),
            jax.ShapeDtypeStruct((views, samples), F32),
        ),
        in_specs=[vmem, vmem],
        out_specs=(vmem, vmem, vmem),
        scratch_shapes=[
            pltpu.VMEM((rows, width), BF16),
            pltpu.VMEM((cols, width), BF16),
            pltpu.VMEM((rows, cols), F32),
            pltpu.VMEM((rows, cols), F32),
            pltpu.VMEM((rows, cols), F32),
            pltpu.VMEM((rows, cols), BF16),
            pltpu.VMEM((views, samples, width), F32),
            pltpu.VMEM((cols, width), F32),
            pltpu.VMEM((rows, LANES), F32),
            pltpu.VMEM((rows, LANES), F32),
            pltpu.VMEM((ITERS, nx, views, cols), F32),
            pltpu.VMEM((5, 2 * ny, 1, rows), F32),
            pltpu.VMEM((5, ny, 1, rows), F32),
            pltpu.VMEM((samples, width), F32),
            pltpu.VMEM((ny, ablock, width), F32),
            pltpu.VMEM((ny, ablock, width), F32),
            pltpu.VMEM((nx, xblock, width), F32),
            pltpu.SemaphoreType.DMA((20, 16)),
            pltpu.SemaphoreType.DMA((20, 16)),
        ],
        compiler_params=pltpu.CompilerParams(
            collective_id=0, has_side_effects=True, vmem_limit_bytes=48 * 2**20
        ),
    )(embeddings.reshape(rows, width), prototypes)
    return ge.reshape(views, samples, width), gp, loss


def solution(mesh):
    nx = mesh.shape["samp"]
    ny = 1
    while 2 * ny * ny < mesh.shape["proto"]:
        ny += 1
    return jax.shard_map(
        functools.partial(body, nx, ny),
        mesh=mesh,
        in_specs=(P(None, "samp", None), P("proto", None)),
        out_specs=(P(None, "samp", None), P("proto", None), P(None, "samp")),
        check_vma=False,
    )
```

time: 1120 us -> 106 us (0.09)
  blocking collectives: 812 us -> 0 us
  waiting for transfers between devices: 270 us -> 0 us
  Pallas kernels: 0 us -> 101 us
  other arithmetic: 17.6 us -> 0 us
  between operations: 14.2 us -> 0.65 us
    psum x6 -> x0, blocking collectives: 812 us -> none  [the longest x3 775 us: body(): totals = lax.psum(jnp.stack([row_sums] + extras), 'proto')]
    psum x2 -> x0, waiting for transfers between devices: 270 us -> none  [the longest x1 197 us: body(): emb_grad = lax.psum(emb_part, 'proto')]
    pallas_call x0 -> x1, Pallas kernels: none -> 101 us  [body(): pl.pallas_call(functools.partial(kernel, nx, ny), out_shape=(jax.ShapeDty...]
  transfers between devices with their start and end apart: 2 -> 0, of which waited for: 2 -> 0; matrix products, arithmetic and copies ran while one was open for 1% -> 0% of each run, Pallas kernels for 0% -> 0%
where the time goes in v1:
time: 106 us
  Pallas kernels  101 us (95%)
  local copies, waits for them, and re-layouts  4.07 us (4%)
    pallas_call x1, Pallas kernels, body(): pl.pallas_call(functools.partial(kernel, nx, ny), out_shape=(jax.ShapeDty...  101 us
    unnamed x7, local copies, waits for them, and re-layouts  4.07 us

profile of v1, /device:TPU:1, one launch (start us, length us, event | category | flops | bytes accessed | tf_op | source)
XLA Modules:
  0.0 105.6 jit_solution(15860322837509763556)
XLA Ops:
  0.6 0.0 copy-start
  0.6 1.0 copy-done
  1.7 0.0 copy-start.1
  1.7 0.9 copy-done.1
  2.6 100.9 %shard_map.49 = (bf16[1024,256]{1,0:T(8,128)(2,1)S(1)}, bf16[512,256]{1,0:T(8,128)(2,1)S(1)}, f32[2,512]{1,0:T(2,128)S(1)}) custom-call(bf16[1024,256]{1,0:T(8,128)(2,1)S(1)} %bitcast.2, bf16[512,256]{1,0:T(8,128)(2,1)S(1)} %copy-done.1), custom_call_target="tpu_custom_call" | custom-call | tf_op jit(solution)/shard_map/pallas_call | solution.py:364
  103.5 0.8 copy.8
  104.3 0.7 copy.9
  105.0 0.6 copy.10
Async XLA Ops:
  0.6 1.0 copy-start
  1.7 0.9 copy-start.1

commit v2 on v0

v2 whole, which is shorter than its diff:
```python
import functools

import jax
import jax.numpy as jnp
from jax import lax
from jax.experimental import pallas as pl
from jax.experimental.pallas import tpu as pltpu
from jax.sharding import PartitionSpec as P

ITERS = 3
INV_TEMPER = 10.0
F32 = jnp.float32
BF16 = jnp.bfloat16
MESH = pl.DeviceIdType.MESH
LANES = 128
SUB = 8


def normalize_rows(values):
    as_float = values.astype(F32)
    inverse = lax.rsqrt(jnp.sum(as_float * as_float, axis=-1, keepdims=True) + 1e-06)
    return as_float * inverse, inverse


def project(summed, unit_rows, inverse):
    return (summed - unit_rows * jnp.sum(unit_rows * summed, axis=-1, keepdims=True)) * inverse


def far_first(count):
    half = count // 2
    order = [half]
    for step in range(1, half + 1):
        for offset in (half - step, half + step):
            if 0 < offset < count and offset not in order:
                order.append(offset)
    return order


def kernel(
    nx,
    ny,
    emb_hbm,
    proto_hbm,
    ge_ref,
    gp_ref,
    loss_ref,
    emb_ref,
    proto_ref,
    eb_ref,
    pb_ref,
    soft_ref,
    sink_ref,
    slope_ref,
    epart_ref,
    ppart_ref,
    wcol_ref,
    tcol_ref,
    scale_ref,
    col_buf,
    row_buf,
    rowz_buf,
    sib_buf,
    a_buf,
    b_buf,
    x_buf,
    load_sem,
    send_sem,
    recv_sem,
    ring_sem,
):
    rows, width = eb_ref.shape
    half = rows // 2
    cols = pb_ref.shape[0]
    tiles = cols // LANES
    x = lax.axis_index("samp")
    p = lax.axis_index("proto")
    y = p // (2 * ny)
    z = (p // 2) % ny
    c = p % 2
    pos = y * 2 + c
    ai = y + (z - y) * c
    bi = z + (y - z) * c
    astep = 2 * ny + (2 - 2 * ny) * c
    bstep = 2 + (2 * ny - 2) * c
    ablock = half // ny
    xblock = cols // nx

    def at_x(j):
        return (j, p)

    def at_yc(j):
        return (x, (j // 2) * (2 * ny) + z * 2 + j % 2)

    def at_z(j):
        return (x, y * (2 * ny) + j * 2 + c)

    def at_a(j):
        return (x, p + (j - ai) * astep)

    def at_b(j):
        return (x, p + (j - bi) * bstep)

    sibling = (x, p + 1 - 2 * c)

    load_proto = pltpu.make_async_copy(proto_hbm, proto_ref, load_sem.at[0])
    load_emb = pltpu.make_async_copy(emb_hbm, emb_ref, load_sem.at[1])
    load_proto.start()
    load_emb.start()

    barrier = pltpu.get_barrier_semaphore()

    def greet(device):
        pl.semaphore_signal(barrier, inc=1, device_id=device, device_id_type=MESH)

    for d in far_first(nx):
        greet(at_x(lax.rem(x + d, nx)))
    for d in far_first(ny):
        for core in range(2):
            greet((x, lax.rem(y + d, ny) * (2 * ny) + z * 2 + core))
        greet((x, y * (2 * ny) + lax.rem(z + d, ny) * 2 + c))
    greet(sibling)
    greetings = nx - 1 + 3 * (ny - 1) + 1

    pending = []

    def sent(stage, ref):
        pending.append(pltpu.make_async_copy(ref, ref, send_sem.at[stage]))

    def flush():
        for copy in pending:
            copy.wait()
        pending.clear()

    def send(stage, source, place, device, received=None):
        pltpu.make_async_remote_copy(
            src_ref=source,
            dst_ref=place,
            send_sem=send_sem.at[stage],
            recv_sem=recv_sem.at[stage] if received is None else received,
            device_id=device,
            device_id_type=MESH,
        ).start()

    def broadcast(stage, count, me, at, buf):
        for d in far_first(count):
            send(stage, buf.at[me], buf.at[me], at(lax.rem(me + d, count)))
        sent(stage, buf.at[pl.ds(0, count - 1)])

    def arrived(stage, ref):
        pltpu.make_async_copy(ref, ref, recv_sem.at[stage]).wait()

    def gathered(stage, count, buf):
        arrived(stage, buf.at[pl.ds(0, count - 1)])

    def total_of(ref, count):
        total = ref[0]
        for j in range(1, count):
            total = total + ref[j]
        return total

    def fold(block):
        return jnp.sum(block.reshape(-1, SUB, LANES), axis=0)

    def across_lanes(block):
        return jnp.sum(fold(block.T), axis=0, keepdims=True)

    def store_columns(ref, tile):
        for r in range(SUB):
            ref[r * LANES : (r + 1) * LANES, :] = jnp.broadcast_to(tile[r : r + 1, :], (LANES, LANES)).T

    lane = [slice(j * LANES, (j + 1) * LANES) for j in range(tiles)]
    step = min(256, half)

    load_proto.wait()
    unit_proto, _ = normalize_rows(proto_ref[...])
    pb_ref[...] = unit_proto.astype(BF16)
    load_emb.wait()
    col = col_buf.at[0]
    for v in range(2):
        sums = [None] * tiles
        for i in range(v * half, (v + 1) * half, step):
            unit, _ = normalize_rows(emb_ref[i : i + step, :])
            eb = unit.astype(BF16)
            eb_ref[i : i + step, :] = eb
            s = lax.dot_general(eb, pb_ref[...], (((1,), (1,)), ((), ())), preferred_element_type=F32)
            soft = jnp.exp(s * INV_TEMPER)
            soft_ref[i : i + step, :] = soft
            for j in range(tiles):
                part = fold(soft[:, lane[j]] * soft[:, lane[j]])
                sums[j] = part if sums[j] is None else sums[j] + part
        for j in range(tiles):
            k = v * tiles + j
            col[x, k : k + 1, :] = jnp.sum(sums[j], axis=0, keepdims=True)

    pl.semaphore_wait(barrier, greetings)

    def row_sums(buf, scale):
        for r in range(SUB):
            v = r // tiles
            block = slice(r * LANES, (r + 1) * LANES)
            total = None
            for j in range(tiles):
                k = v * tiles + j
                part = sink_ref[block, lane[j]] * scale[k : k + 1, :]
                total = part if total is None else total + part
            buf[pos, r : r + 1, :] = across_lanes(total)

    soft_total = None
    weights = None
    scale = None
    extra = row_buf.at[ITERS]
    extraz = rowz_buf.at[ITERS]
    for sweep in range(ITERS):
        col = col_buf.at[sweep]
        if sweep > 0:
            for v in range(2):
                sums = [None] * tiles
                for i in range(v * half, (v + 1) * half, 64):
                    weight = wcol_ref[i : i + 64, :]
                    for j in range(tiles):
                        part = fold(sink_ref[i : i + 64, lane[j]] * weight)
                        sums[j] = part if sums[j] is None else sums[j] + part
                for j in range(tiles):
                    k = v * tiles + j
                    col[x, k : k + 1, :] = jnp.sum(sums[j], axis=0, keepdims=True)
        stage = 3 * sweep
        broadcast(stage, nx, x, at_x, col)
        if sweep == 0:
            for r in range(SUB):
                block = slice(r * LANES, (r + 1) * LANES)
                total = None
                for j in range(tiles):
                    soft = soft_ref[block, lane[j]]
                    sink_ref[block, lane[j]] = soft * soft
                    total = soft if total is None else total + soft
                extra[pos, r : r + 1, :] = across_lanes(total)
            broadcast(9, 2 * ny, pos, at_yc, extra)
        gathered(stage, nx, col)
        scale = 1.0 / total_of(col, nx)
        row = row_buf.at[sweep]
        row_sums(row, scale)
        broadcast(stage + 1, 2 * ny, pos, at_yc, row)
        if sweep == 0:
            gathered(9, 2 * ny, extra)
            extraz[z] = total_of(extra, 2 * ny)
            broadcast(10, ny, z, at_z, extraz)
        gathered(stage + 1, 2 * ny, row)
        rowz = rowz_buf.at[sweep]
        rowz[z] = total_of(row, 2 * ny)
        broadcast(stage + 2, ny, z, at_z, rowz)
        if sweep == 1:
            gathered(10, ny, extraz)
            soft_total = total_of(extraz, ny)
            store_columns(tcol_ref, INV_TEMPER / soft_total)
        if sweep == ITERS - 1:
            scale_ref[...] = scale * INV_TEMPER
        flush()
        gathered(stage + 2, ny, rowz)
        weights = 1.0 / total_of(rowz, ny)
        store_columns(wcol_ref, weights)

    def slopes(v, start):
        mine = pl.multiple_of(v * half + start, step)
        other = pl.multiple_of((1 - v) * half + start, step)
        for i in range(0, step, LANES):
            here = pl.ds(mine + i, LANES)
            there = pl.ds(other + i, LANES)
            weight = wcol_ref[there, :]
            share = tcol_ref[here, :]
            for j in range(tiles):
                pull = sink_ref[there, lane[j]] * scale_ref[pl.ds((1 - v) * tiles + j, 1), :] * weight
                slope_ref[here, lane[j]] = (soft_ref[here, lane[j]] * share - pull).astype(BF16)
        here = pl.ds(mine, step)
        epart_ref[here, :] = jnp.dot(slope_ref[here, :], pb_ref[...], preferred_element_type=F32)

    pieces = half // step
    per_piece = ny // pieces

    def piece(i, index):
        return lax.rem(index // per_piece + 1 + i, pieces)

    for i in range(pieces):
        start = piece(i, bi) * step
        slopes(1 - c, start)
        send(
            11,
            epart_ref.at[pl.ds((1 - c) * half + start, step)],
            sib_buf.at[pl.ds(start, step)],
            sibling,
            ring_sem.at[16 + i],
        )
    sent(11, sib_buf)
    for i in range(pieces):
        slopes(c, piece(i, ai) * step)

    for i in range(pieces):
        which = piece(i, ai)
        part = sib_buf.at[pl.ds(which * step, step)]
        pltpu.make_async_copy(part, part, ring_sem.at[16 + i]).wait()
        part[...] = part[...] + epart_ref[pl.ds(c * half + which * step, step), :]
        for d in range(1 if i == pieces - 1 else 0, per_piece):
            j = which * per_piece + lax.rem(ai + d, per_piece)
            send(13, sib_buf.at[pl.ds(j * ablock, ablock)], a_buf.at[ai], at_a(j))
    sent(13, a_buf.at[pl.ds(0, ny - 1)])
    a_buf[ai] = sib_buf[pl.ds(ai * ablock, ablock), :]

    for k in range(0, cols, LANES):
        ppart_ref[k : k + LANES, :] = lax.dot_general(
            slope_ref[:, k : k + LANES], eb_ref[...], (((0,), (0,)), ((), ())), preferred_element_type=F32
        )
    for d in far_first(nx):
        j = lax.rem(x + d, nx)
        send(12, ppart_ref.at[pl.ds(j * xblock, xblock)], x_buf.at[x], at_x(j))
    sent(12, x_buf.at[pl.ds(0, nx - 1)])
    x_buf[x] = ppart_ref[pl.ds(x * xblock, xblock), :]

    cross = row_buf.at[ITERS + 1]
    for v in range(2):
        for i in range(0, half, step):
            here = slice(v * half + i, v * half + i + step)
            s = lax.dot_general(
                eb_ref[here, :], pb_ref[...], (((1,), (1,)), ((), ())), preferred_element_type=F32
            )
            for q in range(0, step, LANES):
                other = slice((1 - v) * half + i + q, (1 - v) * half + i + q + LANES)
                total = None
                for j in range(tiles):
                    k = (1 - v) * tiles + j
                    part = sink_ref[other, lane[j]] * scale_ref[k : k + 1, :] * s[q : q + LANES, lane[j]]
                    total = part if total is None else total + part
                r = (v * half + i + q) // LANES
                cross[pos, r : r + 1, :] = across_lanes(total)
    broadcast(14, 2 * ny, pos, at_yc, cross)

    gathered(13, ny, a_buf)
    b_buf[bi] = total_of(a_buf, ny)
    broadcast(15, ny, bi, at_b, b_buf)

    crossz = rowz_buf.at[ITERS + 1]
    gathered(14, 2 * ny, cross)
    crossz[z] = total_of(cross, 2 * ny)
    broadcast(16, ny, z, at_z, crossz)

    own = pl.ds(x * xblock, xblock)
    unit, inverse = normalize_rows(proto_ref[own, :])
    gathered(12, nx, x_buf)
    gp_ref[own, :] = project(total_of(x_buf, nx), unit, inverse).astype(BF16)
    for d in far_first(nx):
        send(17, gp_ref.at[own], gp_ref.at[own], at_x(lax.rem(x + d, nx)))
    sent(17, gp_ref.at[pl.ds(0, (nx - 1) * xblock)])

    own = pl.ds(c * half + ai * ablock, ablock)
    unit, inverse = normalize_rows(emb_ref[own, :])
    gathered(15, ny, b_buf)
    ge_ref[own, :] = project(total_of(b_buf, ny), unit, inverse).astype(BF16)
    for d in far_first(ny):
        send(18, ge_ref.at[own], ge_ref.at[own], at_a(lax.rem(ai + d, ny)), ring_sem.at[ai])
    sent(18, ge_ref.at[pl.ds(0, (ny - 1) * ablock)])
    send(19, ge_ref.at[own], ge_ref.at[own], sibling)

    gathered(16, ny, crossz)
    swapped = jnp.concatenate([weights[tiles:], weights[:tiles]], axis=0)
    loss = jnp.log(soft_total) - total_of(crossz, ny) * swapped
    for v in range(2):
        for j in range(tiles):
            loss_ref[v : v + 1, lane[j]] = loss[v * tiles + j : v * tiles + j + 1, :]

    for d in reversed(far_first(ny)):
        j = lax.rem(ai + d, ny)
        block = ge_ref.at[pl.ds(c * half + j * ablock, ablock)]
        pltpu.make_async_copy(block, block, ring_sem.at[j]).wait()
        send(19, block, block, sibling)
    sent(19, ge_ref.at[pl.ds(0, half)])
    arrived(17, gp_ref.at[pl.ds(0, (nx - 1) * xblock)])
    flush()
    arrived(19, ge_ref.at[pl.ds(0, half)])


def finish(ge_ref, gp_ref, loss_ref, ge_out, gp_out, loss_out, sem):
    copies = [
        pltpu.make_async_copy(ge_ref, ge_out, sem.at[0]),
        pltpu.make_async_copy(gp_ref, gp_out, sem.at[1]),
        pltpu.make_async_copy(loss_ref, loss_out, sem.at[2]),
    ]
    for copy in copies:
        copy.start()
    for copy in copies:
        copy.wait()


def body(nx, ny, embeddings, prototypes):
    views, samples, width = embeddings.shape
    rows, cols = views * samples, prototypes.shape[0]
    ablock, xblock = samples // ny, cols // nx
    vmem = pl.BlockSpec(memory_space=pltpu.VMEM)
    hbm = pl.BlockSpec(memory_space=pltpu.HBM)
    shapes = (
        jax.ShapeDtypeStruct((rows, width), BF16),
        jax.ShapeDtypeStruct((cols, width), BF16),
        jax.ShapeDtypeStruct((views, samples), F32),
    )
    results = pl.pallas_call(
        functools.partial(kernel, nx, ny),
        out_shape=shapes,
        in_specs=[hbm, hbm],
        out_specs=(vmem, vmem, vmem),
        scratch_shapes=[
            pltpu.VMEM((rows, width), BF16),
            pltpu.VMEM((cols, width), BF16),
            pltpu.VMEM((rows, width), BF16),
            pltpu.VMEM((cols, width), BF16),
            pltpu.VMEM((rows, cols), F32),
            pltpu.VMEM((rows, cols), F32),
            pltpu.VMEM((rows, cols), BF16),
            pltpu.VMEM((rows, width), F32),
            pltpu.VMEM((cols, width), F32),
            pltpu.VMEM((rows, LANES), F32),
            pltpu.VMEM((rows, LANES), F32),
            pltpu.VMEM((SUB, LANES), F32),
            pltpu.VMEM((ITERS, nx, SUB, LANES), F32),
            pltpu.VMEM((ITERS + 2, 2 * ny, SUB, LANES), F32),
            pltpu.VMEM((ITERS + 2, ny, SUB, LANES), F32),
            pltpu.VMEM((samples, width), F32),
            pltpu.VMEM((ny, ablock, width), F32),
            pltpu.VMEM((ny, ablock, width), F32),
            pltpu.VMEM((nx, xblock, width), F32),
            pltpu.SemaphoreType.DMA((2,)),
            pltpu.SemaphoreType.DMA((20,)),
            pltpu.SemaphoreType.DMA((20,)),
            pltpu.SemaphoreType.DMA((24,)),
        ],
        compiler_params=pltpu.CompilerParams(
            collective_id=0, has_side_effects=True, vmem_limit_bytes=48 * 2**20
        ),
    )(embeddings.reshape(rows, width), prototypes)
    ge, gp, loss = pl.pallas_call(
        finish,
        out_shape=shapes,
        in_specs=[vmem, vmem, vmem],
        out_specs=(hbm, hbm, hbm),
        scratch_shapes=[pltpu.SemaphoreType.DMA((3,))],
        compiler_params=pltpu.CompilerParams(vmem_limit_bytes=8 * 2**20),
    )(*results)
    return ge.reshape(views, samples, width), gp, loss


def solution(mesh):
    nx = mesh.shape["samp"]
    ny = 1
    while 2 * ny * ny < mesh.shape["proto"]:
        ny += 1
    return jax.shard_map(
        functools.partial(body, nx, ny),
        mesh=mesh,
        in_specs=(P(None, "samp", None), P("proto", None)),
        out_specs=(P(None, "samp", None), P("proto", None), P(None, "samp")),
        check_vma=False,
    )
```

time: 1120 us -> 98.9 us (0.09)
  blocking collectives: 812 us -> 0 us
  waiting for transfers between devices: 270 us -> 0 us
  Pallas kernels: 0 us -> 96.1 us
  other arithmetic: 17.6 us -> 0 us
  between operations: 14.2 us -> 0.65 us
    psum x6 -> x0, blocking collectives: 812 us -> none  [the longest x3 775 us: body(): totals = lax.psum(jnp.stack([row_sums] + extras), 'proto')]
    psum x2 -> x0, waiting for transfers between devices: 270 us -> none  [the longest x1 197 us: body(): emb_grad = lax.psum(emb_part, 'proto')]
    pallas_call x0 -> x2, Pallas kernels: none -> 96.1 us  [the longest x1 95.1 us: body(): pl.pallas_call(functools.partial(kernel, nx, ny), out_shape=shapes, in_sp...]
  transfers between devices with their start and end apart: 2 -> 0, of which waited for: 2 -> 0; matrix products, arithmetic and copies ran while one was open for 1% -> 0% of each run, Pallas kernels for 0% -> 0%
where the time goes in v2:
time: 98.9 us; the launch traced here: 98.7 us
  Pallas kernels  96.1 us (97%)
  local copies, waits for them, and re-layouts  1.98 us (2%)
    pallas_call x1, Pallas kernels, body(): pl.pallas_call(functools.partial(kernel, nx, ny), out_shape=shapes, in_sp...  95.1 us
    unnamed x4, local copies, waits for them, and re-layouts  1.98 us

profile of v2, /device:TPU:1, one launch (start us, length us, event | category | flops | bytes accessed | tf_op | source)
XLA Modules:
  0.0 98.7 jit_solution(11807332391987855119)
XLA Ops:
  0.6 0.0 copy-start
  0.6 1.0 %copy-done = bf16[2,512,256]{2,1,0:T(8,128)(2,1)S(1)} copy-done((bf16[2,512,256]{2,1,0:T(8,128)(2,1)S(1)}, bf16[2,512,256]{2,1,0:T(8,128)(2,1)}, u32[]{:S(2)}) %copy-start) | copy-done | bytes 524312
  1.7 0.0 copy-start.1
  1.7 0.9 copy-done.1
  2.6 95.1 %shard_map.49 = (bf16[1024,256]{1,0:T(8,128)(2,1)S(1)}, bf16[512,256]{1,0:T(8,128)(2,1)S(1)}, f32[2,512]{1,0:T(2,128)S(1)}) custom-call(bf16[1024,256]{1,0:T(8,128)(2,1)S(1)} %bitcast.2, bf16[512,256]{1,0:T(8,128)(2,1)S(1)} %copy-done.1), custom_call_target="tpu_custom_call" | custom-call | tf_op jit(solution)/shard_map/pallas_call | solution.py:402
  97.8 0.9 shard_map.50
Async XLA Ops:
  0.6 1.0 %copy-start = (bf16[2,512,256]{2,1,0:T(8,128)(2,1)S(1)}, bf16[2,512,256]{2,1,0:T(8,128)(2,1)}, u32[]{:S(2)}) copy-start(bf16[2,512,256]{2,1,0:T(8,128)(2,1)} %param.2) | copy-start | bytes 1572868
  1.7 0.9 copy-start.1

commit v3 on v2

--- a/solution.py
+++ b/solution.py
@@ -14,6 +14,16 @@
 MESH = pl.DeviceIdType.MESH
 LANES = 128
 SUB = 8
+SOFT = 9
+SIBLING_SUM = 11
+PROTO_RS = 13
+PROTO_AG = 15
+EMB_A = 17
+EMB_B = 19
+EMB_AG = 21
+TO_SIBLING = 23
+CROSS = 25
+STAGES = 27
 
 
 def normalize_rows(values):
@@ -82,8 +92,10 @@
     bi = z + (y - z) * c
     astep = 2 * ny + (2 - 2 * ny) * c
     bstep = 2 + (2 * ny - 2) * c
-    ablock = half // ny
-    xblock = cols // nx
+    step = half // 2
+    xstep = cols // 2
+    aq = step // ny
+    xq = xstep // nx
 
     def at_x(j):
         return (j, p)
@@ -169,7 +181,6 @@
             ref[r * LANES : (r + 1) * LANES, :] = jnp.broadcast_to(tile[r : r + 1, :], (LANES, LANES)).T
 
     lane = [slice(j * LANES, (j + 1) * LANES) for j in range(tiles)]
-    step = min(256, half)
 
     load_proto.wait()
     unit_proto, _ = normalize_rows(proto_ref[...])
@@ -234,22 +245,22 @@
                     sink_ref[block, lane[j]] = soft * soft
                     total = soft if total is None else total + soft
                 extra[pos, r : r + 1, :] = across_lanes(total)
-            broadcast(9, 2 * ny, pos, at_yc, extra)
+            broadcast(SOFT, 2 * ny, pos, at_yc, extra)
         gathered(stage, nx, col)
         scale = 1.0 / total_of(col, nx)
         row = row_buf.at[sweep]
         row_sums(row, scale)
         broadcast(stage + 1, 2 * ny, pos, at_yc, row)
         if sweep == 0:
-            gathered(9, 2 * ny, extra)
+            gathered(SOFT, 2 * ny, extra)
             extraz[z] = total_of(extra, 2 * ny)
-            broadcast(10, ny, z, at_z, extraz)
+            broadcast(SOFT + 1, ny, z, at_z, extraz)
         gathered(stage + 1, 2 * ny, row)
         rowz = rowz_buf.at[sweep]
         rowz[z] = total_of(row, 2 * ny)
         broadcast(stage + 2, ny, z, at_z, rowz)
         if sweep == 1:
-            gathered(10, ny, extraz)
+            gathered(SOFT + 1, ny, extraz)
             soft_total = total_of(extraz, ny)
             store_columns(tcol_ref, INV_TEMPER / soft_total)
         if sweep == ITERS - 1:
@@ -259,9 +270,9 @@
         weights = 1.0 / total_of(rowz, ny)
         store_columns(wcol_ref, weights)
 
-    def slopes(v, start):
-        mine = pl.multiple_of(v * half + start, step)
-        other = pl.multiple_of((1 - v) * half + start, step)
+    def slopes(v, h):
+        mine = pl.multiple_of(v * half + h * step, step)
+        other = pl.multiple_of((1 - v) * half + h * step, step)
         for i in range(0, step, LANES):
             here = pl.ds(mine + i, LANES)
             there = pl.ds(other + i, LANES)
@@ -273,46 +284,55 @@
         here = pl.ds(mine, step)
         epart_ref[here, :] = jnp.dot(slope_ref[here, :], pb_ref[...], preferred_element_type=F32)
 
-    pieces = half // step
-    per_piece = ny // pieces
-
-    def piece(i, index):
-        return lax.rem(index // per_piece + 1 + i, pieces)
-
-    for i in range(pieces):
-        start = piece(i, bi) * step
-        slopes(1 - c, start)
-        send(
-            11,
-            epart_ref.at[pl.ds((1 - c) * half + start, step)],
-            sib_buf.at[pl.ds(start, step)],
-            sibling,
-            ring_sem.at[16 + i],
-        )
-    sent(11, sib_buf)
-    for i in range(pieces):
-        slopes(c, piece(i, ai) * step)
-
-    for i in range(pieces):
-        which = piece(i, ai)
-        part = sib_buf.at[pl.ds(which * step, step)]
-        pltpu.make_async_copy(part, part, ring_sem.at[16 + i]).wait()
-        part[...] = part[...] + epart_ref[pl.ds(c * half + which * step, step), :]
-        for d in range(1 if i == pieces - 1 else 0, per_piece):
-            j = which * per_piece + lax.rem(ai + d, per_piece)
-            send(13, sib_buf.at[pl.ds(j * ablock, ablock)], a_buf.at[ai], at_a(j))
-    sent(13, a_buf.at[pl.ds(0, ny - 1)])
-    a_buf[ai] = sib_buf[pl.ds(ai * ablock, ablock), :]
-
-    for k in range(0, cols, LANES):
-        ppart_ref[k : k + LANES, :] = lax.dot_general(
-            slope_ref[:, k : k + LANES], eb_ref[...], (((0,), (0,)), ((), ())), preferred_element_type=F32
-        )
-    for d in far_first(nx):
-        j = lax.rem(x + d, nx)
-        send(12, ppart_ref.at[pl.ds(j * xblock, xblock)], x_buf.at[x], at_x(j))
-    sent(12, x_buf.at[pl.ds(0, nx - 1)])
-    x_buf[x] = ppart_ref[pl.ds(x * xblock, xblock), :]
+    def proto_terms(h):
+        for k in range(h * xstep, (h + 1) * xstep, LANES):
+            ppart_ref[k : k + LANES, :] = lax.dot_general(
+                slope_ref[:, k : k + LANES], eb_ref[...], (((0,), (0,)), ((), ())), preferred_element_type=F32
+            )
+        for d in far_first(nx):
+            j = lax.rem(x + d, nx)
+            send(PROTO_RS + h, ppart_ref.at[pl.ds(h * xstep + j * xq, xq)], x_buf.at[h, x], at_x(j))
+        sent(PROTO_RS + h, x_buf.at[h, pl.ds(0, nx - 1)])
+        x_buf[h, x] = ppart_ref[pl.ds(h * xstep + x * xq, xq), :]
+
+    def proto_result(h):
+        own = pl.ds(h * xstep + x * xq, xq)
+        unit, inverse = normalize_rows(proto_ref[own, :])
+        gathered(PROTO_RS + h, nx, x_buf.at[h])
+        gp_ref[own, :] = project(total_of(x_buf.at[h], nx), unit, inverse).astype(BF16)
+        for d in far_first(nx):
+            send(PROTO_AG + h, gp_ref.at[own], gp_ref.at[own], at_x(lax.rem(x + d, nx)))
+        sent(PROTO_AG + h, gp_ref.at[pl.ds(0, (nx - 1) * xq)])
+
+    def emb_result(h):
+        own = pl.ds(c * half + h * step + ai * aq, aq)
+        unit, inverse = normalize_rows(emb_ref[own, :])
+        gathered(EMB_B + h, ny, b_buf.at[h])
+        ge_ref[own, :] = project(total_of(b_buf.at[h], ny), unit, inverse).astype(BF16)
+        block = ge_ref.at[own]
+        for d in far_first(ny):
+            send(EMB_AG + h, block, block, at_a(lax.rem(ai + d, ny)), ring_sem.at[h, ai])
+        sent(EMB_AG + h, ge_ref.at[pl.ds(0, (ny - 1) * aq)])
+        send(TO_SIBLING + h, block, block, sibling)
+
+    for h in range(2):
+        slopes(1 - c, h)
+        part = pl.ds(h * step, step)
+        send(SIBLING_SUM + h, epart_ref.at[pl.ds((1 - c) * half + h * step, step)], sib_buf.at[part], sibling)
+        sent(SIBLING_SUM + h, sib_buf.at[part])
+    for h in range(2):
+        slopes(c, h)
+    proto_terms(0)
+    for h in range(2):
+        part = pl.ds(h * step, step)
+        arrived(SIBLING_SUM + h, sib_buf.at[part])
+        sib_buf[part, :] = sib_buf[part, :] + epart_ref[pl.ds(c * half + h * step, step), :]
+        for d in far_first(ny):
+            j = lax.rem(ai + d, ny)
+            send(EMB_A + h, sib_buf.at[pl.ds(h * step + j * aq, aq)], a_buf.at[h, ai], at_a(j))
+        sent(EMB_A + h, a_buf.at[h, pl.ds(0, ny - 1)])
+        a_buf[h, ai] = sib_buf[pl.ds(h * step + ai * aq, aq), :]
+    proto_terms(1)
 
     cross = row_buf.at[ITERS + 1]
     for v in range(2):
@@ -330,50 +350,41 @@
                     total = part if total is None else total + part
                 r = (v * half + i + q) // LANES
                 cross[pos, r : r + 1, :] = across_lanes(total)
-    broadcast(14, 2 * ny, pos, at_yc, cross)
-
-    gathered(13, ny, a_buf)
-    b_buf[bi] = total_of(a_buf, ny)
-    broadcast(15, ny, bi, at_b, b_buf)
-
+    broadcast(CROSS, 2 * ny, pos, at_yc, cross)
+
+    for h in range(2):
+        gathered(EMB_A + h, ny, a_buf.at[h])
+        b_buf[h, bi] = total_of(a_buf.at[h], ny)
+        broadcast(EMB_B + h, ny, bi, at_b, b_buf.at[h])
+
+    proto_result(0)
     crossz = rowz_buf.at[ITERS + 1]
-    gathered(14, 2 * ny, cross)
+    gathered(CROSS, 2 * ny, cross)
     crossz[z] = total_of(cross, 2 * ny)
-    broadcast(16, ny, z, at_z, crossz)
-
-    own = pl.ds(x * xblock, xblock)
-    unit, inverse = normalize_rows(proto_ref[own, :])
-    gathered(12, nx, x_buf)
-    gp_ref[own, :] = project(total_of(x_buf, nx), unit, inverse).astype(BF16)
-    for d in far_first(nx):
-        send(17, gp_ref.at[own], gp_ref.at[own], at_x(lax.rem(x + d, nx)))
-    sent(17, gp_ref.at[pl.ds(0, (nx - 1) * xblock)])
-
-    own = pl.ds(c * half + ai * ablock, ablock)
-    unit, inverse = normalize_rows(emb_ref[own, :])
-    gathered(15, ny, b_buf)
-    ge_ref[own, :] = project(total_of(b_buf, ny), unit, inverse).astype(BF16)
-    for d in far_first(ny):
-        send(18, ge_ref.at[own], ge_ref.at[own], at_a(lax.rem(ai + d, ny)), ring_sem.at[ai])
-    sent(18, ge_ref.at[pl.ds(0, (ny - 1) * ablock)])
-    send(19, ge_ref.at[own], ge_ref.at[own], sibling)
-
-    gathered(16, ny, crossz)
+    broadcast(CROSS + 1, ny, z, at_z, crossz)
+    emb_result(0)
+    proto_result(1)
+    emb_result(1)
+
+    gathered(CROSS + 1, ny, crossz)
     swapped = jnp.concatenate([weights[tiles:], weights[:tiles]], axis=0)
     loss = jnp.log(soft_total) - total_of(crossz, ny) * swapped
     for v in range(2):
         for j in range(tiles):
             loss_ref[v : v + 1, lane[j]] = loss[v * tiles + j : v * tiles + j + 1, :]
 
-    for d in reversed(far_first(ny)):
-        j = lax.rem(ai + d, ny)
-        block = ge_ref.at[pl.ds(c * half + j * ablock, ablock)]
-        pltpu.make_async_copy(block, block, ring_sem.at[j]).wait()
-        send(19, block, block, sibling)
-    sent(19, ge_ref.at[pl.ds(0, half)])
-    arrived(17, gp_ref.at[pl.ds(0, (nx - 1) * xblock)])
+    for h in range(2):
+        for d in reversed(far_first(ny)):
+            j = lax.rem(ai + d, ny)
+            block = ge_ref.at[pl.ds(c * half + h * step + j * aq, aq)]
+            pltpu.make_async_copy(block, block, ring_sem.at[h, j]).wait()
+            send(TO_SIBLING + h, block, block, sibling)
+        sent(TO_SIBLING + h, ge_ref.at[pl.ds(0, step)])
+    for h in range(2):
+        arrived(PROTO_AG + h, gp_ref.at[pl.ds(0, (nx - 1) * xq)])
     flush()
-    arrived(19, ge_ref.at[pl.ds(0, half)])
+    for h in range(2):
+        arrived(TO_SIBLING + h, ge_ref.at[pl.ds(0, step)])
 
 
 def finish(ge_ref, gp_ref, loss_ref, ge_out, gp_out, loss_out, sem):
@@ -391,7 +402,7 @@
 def body(nx, ny, embeddings, prototypes):
     views, samples, width = embeddings.shape
     rows, cols = views * samples, prototypes.shape[0]
-    ablock, xblock = samples // ny, cols // nx
+    aq, xq = samples // 2 // ny, cols // 2 // nx
     vmem = pl.BlockSpec(memory_space=pltpu.VMEM)
     hbm = pl.BlockSpec(memory_space=pltpu.HBM)
     shapes = (
@@ -421,18 +432,21 @@
             pltpu.VMEM((ITERS + 2, 2 * ny, SUB, LANES), F32),
             pltpu.VMEM((ITERS + 2, ny, SUB, LANES), F32),
             pltpu.VMEM((samples, width), F32),
-            pltpu.VMEM((ny, ablock, width), F32),
-            pltpu.VMEM((ny, ablock, width), F32),
-            pltpu.VMEM((nx, xblock, width), F32),
+            pltpu.VMEM((2, ny, aq, width), F32),
+            pltpu.VMEM((2, ny, aq, width), F32),
+            pltpu.VMEM((2, nx, xq, width), F32),
             pltpu.SemaphoreType.DMA((2,)),
-            pltpu.SemaphoreType.DMA((20,)),
-            pltpu.SemaphoreType.DMA((20,)),
-            pltpu.SemaphoreType.DMA((24,)),
+            pltpu.SemaphoreType.DMA((STAGES,)),
+            pltpu.SemaphoreType.DMA((STAGES,)),
+            pltpu.SemaphoreType.DMA((2, ny)),
         ],
         compiler_params=pltpu.CompilerParams(
             collective_id=0, has_side_effects=True, vmem_limit_bytes=48 * 2**20
         ),
-    )(embeddings.reshape(rows, width), prototypes)
+    )(
+        pltpu.with_memory_space_constraint(embeddings.reshape(rows, width), pltpu.HBM),
+        pltpu.with_memory_space_constraint(prototypes, pltpu.HBM),
+    )
     ge, gp, loss = pl.pallas_call(
         finish,
         out_shape=shapes,

time: 98.9 us -> 95.5 us (0.966)
  local copies, waits for them, and re-layouts: 1.98 us -> 0 us
  Pallas kernels: 96.1 us -> 94.7 us
    unnamed x4 -> x0, local copies, waits for them, and re-layouts: 1.98 us -> none
    pallas_call x1, Pallas kernels: 95.1 us -> 93.8 us  [body(): pl.pallas_call(functools.partial(kernel, nx, ny), out_shape=shapes, in_sp...]
where the time goes in v3:
time: 95.5 us; the launch traced here: 95.4 us
  Pallas kernels  94.7 us (99%)
    pallas_call x1, Pallas kernels, body(): pl.pallas_call(functools.partial(kernel, nx, ny), out_shape=shapes, in_sp...  93.8 us

profile of v3, /device:TPU:1, one launch (start us, length us, event | category | flops | bytes accessed | tf_op | source)
XLA Modules:
  0.0 95.4 jit_solution(9849908049530896993)
XLA Ops:
  0.6 93.8 %shard_map.49 = (bf16[1024,256]{1,0:T(8,128)(2,1)S(1)}, bf16[512,256]{1,0:T(8,128)(2,1)S(1)}, f32[2,512]{1,0:T(2,128)S(1)}) custom-call(bf16[1024,256]{1,0:T(8,128)(2,1)} %bitcast.2, bf16[512,256]{1,0:T(8,128)(2,1)} %proto_hbm.1), custom_call_target="tpu_custom_call" | custom-call | tf_op jit(solution)/shard_map/pallas_call | solution.py:413
  94.5 0.9 shard_map.50

commit v4 on v3

--- a/solution.py
+++ b/solution.py
@@ -15,15 +15,16 @@
 LANES = 128
 SUB = 8
 SOFT = 9
-SIBLING_SUM = 11
-PROTO_RS = 13
-PROTO_AG = 15
-EMB_A = 17
-EMB_B = 19
-EMB_AG = 21
-TO_SIBLING = 23
-CROSS = 25
-STAGES = 27
+PROTO_RS = 11
+PROTO_AG = 13
+EMB_B = 15
+EMB_AG = 17
+TO_SIBLING = 19
+CROSS = 21
+SCALES = 23
+PAIR = 24
+RING = 25
+STAGES = 29
 
 
 def normalize_rows(values):
@@ -61,7 +62,10 @@
     soft_ref,
     sink_ref,
     slope_ref,
-    epart_ref,
+    ring_ref,
+    ring_soft,
+    ring_sink,
+    ring_slope,
     ppart_ref,
     wcol_ref,
     tcol_ref,
@@ -69,14 +73,14 @@
     col_buf,
     row_buf,
     rowz_buf,
-    sib_buf,
-    a_buf,
+    scales_buf,
     b_buf,
     x_buf,
     load_sem,
     send_sem,
     recv_sem,
     ring_sem,
+    block_sem,
 ):
     rows, width = eb_ref.shape
     half = rows // 2
@@ -129,9 +133,9 @@
     for d in far_first(ny):
         for core in range(2):
             greet((x, lax.rem(y + d, ny) * (2 * ny) + z * 2 + core))
-        greet((x, y * (2 * ny) + lax.rem(z + d, ny) * 2 + c))
+            greet((x, y * (2 * ny) + lax.rem(z + d, ny) * 2 + core))
     greet(sibling)
-    greetings = nx - 1 + 3 * (ny - 1) + 1
+    greetings = nx - 1 + 4 * (ny - 1) + 1
 
     pending = []
 
@@ -185,6 +189,7 @@
     load_proto.wait()
     unit_proto, _ = normalize_rows(proto_ref[...])
     pb_ref[...] = unit_proto.astype(BF16)
+    ring_ref[ai, pl.ds(pl.multiple_of(c * cols, cols), cols), :] = pb_ref[...]
     load_emb.wait()
     col = col_buf.at[0]
     for v in range(2):
@@ -204,6 +209,43 @@
             col[x, k : k + 1, :] = jnp.sum(sums[j], axis=0, keepdims=True)
 
     pl.semaphore_wait(barrier, greetings)
+
+    right = lax.rem(ai + 1, ny)
+    left = lax.rem(ai + ny - 1, ny)
+
+    def slot(offset):
+        return lax.rem(ai + offset + ny, ny)
+
+    def pass_on(hop):
+        back, ahead = slot(-hop), slot(hop)
+        if hop < ny // 2 - 1:
+            send(RING + hop, ring_ref.at[back], ring_ref.at[back], at_a(right), ring_sem.at[back])
+            send(RING + hop, ring_ref.at[ahead], ring_ref.at[ahead], at_a(left), ring_sem.at[ahead])
+            sent(RING + hop, ring_ref.at[pl.ds(0, 2)])
+        else:
+            for to, origin, half_of in ((right, back, 0), (left, ahead, 1)):
+                block = ring_ref.at[origin, pl.ds(half_of * cols, cols)]
+                send(RING + hop, block, block, at_a(to), ring_sem.at[origin])
+            sent(RING + hop, ring_ref.at[0])
+
+    def passed(offset):
+        block = ring_ref.at[slot(offset)]
+        pltpu.make_async_copy(block, block, ring_sem.at[slot(offset)]).wait()
+
+    def ring_terms(offset):
+        mine = eb_ref[pl.ds(pl.multiple_of(c * half + ai * 2 * aq, 2 * aq), 2 * aq), :]
+        other = eb_ref[pl.ds(pl.multiple_of((1 - c) * half + ai * 2 * aq, 2 * aq), 2 * aq), :]
+        both = jnp.concatenate([mine, other], axis=0)
+        for k in range(0, 2 * cols, cols):
+            s = lax.dot_general(
+                both,
+                ring_ref[slot(offset), k : k + cols, :],
+                (((1,), (1,)), ((), ())),
+                preferred_element_type=F32,
+            )
+            soft = jnp.exp(s * INV_TEMPER)
+            ring_soft[offset % ny, :, k : k + cols] = soft[: 2 * aq]
+            ring_sink[offset % ny, :, k : k + cols] = soft[2 * aq :] * soft[2 * aq :]
 
     def row_sums(buf, scale):
         for r in range(SUB):
@@ -237,6 +279,19 @@
         stage = 3 * sweep
         broadcast(stage, nx, x, at_x, col)
         if sweep == 0:
+            pair = ring_ref.at[ai, pl.ds(c * cols, cols)]
+            send(PAIR, pair, ring_ref.at[bi, pl.ds(c * cols, cols)], sibling)
+            sent(PAIR, pb_ref)
+        if sweep == 1:
+            ring_terms(1)
+            ring_terms(-1)
+        if sweep == 2:
+            passed(3)
+            passed(-3)
+            pass_on(3)
+            ring_terms(3)
+            ring_terms(-3)
+        if sweep == 0:
             for r in range(SUB):
                 block = slice(r * LANES, (r + 1) * LANES)
                 total = None
@@ -246,6 +301,8 @@
                     total = soft if total is None else total + soft
                 extra[pos, r : r + 1, :] = across_lanes(total)
             broadcast(SOFT, 2 * ny, pos, at_yc, extra)
+            arrived(PAIR, pb_ref)
+            pass_on(0)
         gathered(stage, nx, col)
         scale = 1.0 / total_of(col, nx)
         row = row_buf.at[sweep]
@@ -255,6 +312,20 @@
             gathered(SOFT, 2 * ny, extra)
             extraz[z] = total_of(extra, 2 * ny)
             broadcast(SOFT + 1, ny, z, at_z, extraz)
+            ring_terms(0)
+        if sweep == 1:
+            passed(2)
+            passed(-2)
+            pass_on(2)
+        if sweep == 2:
+            tens = scale * INV_TEMPER
+            scale_ref[...] = tens
+            scales_buf[ai * 2 + c] = tens
+            for d in far_first(ny):
+                send(SCALES, scale_ref, scales_buf.at[y * 2 + c], (x, lax.rem(y + d, ny) * (2 * ny) + z * 2))
+                send(SCALES, scale_ref, scales_buf.at[z * 2 + c], (x, y * (2 * ny) + lax.rem(z + d, ny) * 2 + 1))
+            send(SCALES, scale_ref, scales_buf.at[bi * 2 + c], sibling)
+            sent(SCALES, scales_buf.at[pl.ds(0, 2 * ny - 1)])
         gathered(stage + 1, 2 * ny, row)
         rowz = rowz_buf.at[sweep]
         rowz[z] = total_of(row, 2 * ny)
@@ -263,9 +334,17 @@
             gathered(SOFT + 1, ny, extraz)
             soft_total = total_of(extraz, ny)
             store_columns(tcol_ref, INV_TEMPER / soft_total)
-        if sweep == ITERS - 1:
-            scale_ref[...] = scale * INV_TEMPER
-        flush()
+            ring_terms(2)
+            ring_terms(-2)
+        if sweep == 0:
+            passed(1)
+            passed(-1)
+            pass_on(1)
+        if sweep == 2:
+            passed(4)
+            ring_terms(4)
+            gathered(SCALES, 2 * ny, scales_buf)
+            flush()
         gathered(stage + 2, ny, rowz)
         weights = 1.0 / total_of(rowz, ny)
         store_columns(wcol_ref, weights)
@@ -281,8 +360,6 @@
             for j in range(tiles):
                 pull = sink_ref[there, lane[j]] * scale_ref[pl.ds((1 - v) * tiles + j, 1), :] * weight
                 slope_ref[here, lane[j]] = (soft_ref[here, lane[j]] * share - pull).astype(BF16)
-        here = pl.ds(mine, step)
-        epart_ref[here, :] = jnp.dot(slope_ref[here, :], pb_ref[...], preferred_element_type=F32)
 
     def proto_terms(h):
         for k in range(h * xstep, (h + 1) * xstep, LANES):
@@ -305,33 +382,35 @@
         sent(PROTO_AG + h, gp_ref.at[pl.ds(0, (nx - 1) * xq)])
 
     def emb_result(h):
-        own = pl.ds(c * half + h * step + ai * aq, aq)
+        own = pl.ds(c * half + (2 * ai + h) * aq, aq)
         unit, inverse = normalize_rows(emb_ref[own, :])
         gathered(EMB_B + h, ny, b_buf.at[h])
         ge_ref[own, :] = project(total_of(b_buf.at[h], ny), unit, inverse).astype(BF16)
         block = ge_ref.at[own]
         for d in far_first(ny):
-            send(EMB_AG + h, block, block, at_a(lax.rem(ai + d, ny)), ring_sem.at[h, ai])
+            send(EMB_AG + h, block, block, at_a(lax.rem(ai + d, ny)), block_sem.at[h, ai])
         sent(EMB_AG + h, ge_ref.at[pl.ds(0, (ny - 1) * aq)])
         send(TO_SIBLING + h, block, block, sibling)
 
+    share = tcol_ref[pl.ds(pl.multiple_of(c * half + ai * 2 * aq, 2 * aq), 2 * aq), :]
+    weight = wcol_ref[pl.ds(pl.multiple_of((1 - c) * half + ai * 2 * aq, 2 * aq), 2 * aq), :]
+    total = None
+    for offset in range(ny):
+        for k in range(2 * tiles):
+            at = slice(k * LANES, (k + 1) * LANES)
+            factor = scales_buf[slot(offset) * 2 + k // tiles, pl.ds((1 - c) * tiles + k % tiles, 1), :]
+            pull = ring_sink[offset, :, at] * factor * weight
+            ring_slope[offset, :, at] = (ring_soft[offset, :, at] * share - pull).astype(BF16)
+        part = jnp.dot(ring_slope[offset], ring_ref[slot(offset)], preferred_element_type=F32)
+        total = part if total is None else total + part
     for h in range(2):
-        slopes(1 - c, h)
-        part = pl.ds(h * step, step)
-        send(SIBLING_SUM + h, epart_ref.at[pl.ds((1 - c) * half + h * step, step)], sib_buf.at[part], sibling)
-        sent(SIBLING_SUM + h, sib_buf.at[part])
-    for h in range(2):
-        slopes(c, h)
+        b_buf[h, bi] = total[h * aq : (h + 1) * aq]
+        broadcast(EMB_B + h, ny, bi, at_b, b_buf.at[h])
+
+    for v in range(2):
+        for h in range(2):
+            slopes(v, h)
     proto_terms(0)
-    for h in range(2):
-        part = pl.ds(h * step, step)
-        arrived(SIBLING_SUM + h, sib_buf.at[part])
-        sib_buf[part, :] = sib_buf[part, :] + epart_ref[pl.ds(c * half + h * step, step), :]
-        for d in far_first(ny):
-            j = lax.rem(ai + d, ny)
-            send(EMB_A + h, sib_buf.at[pl.ds(h * step + j * aq, aq)], a_buf.at[h, ai], at_a(j))
-        sent(EMB_A + h, a_buf.at[h, pl.ds(0, ny - 1)])
-        a_buf[h, ai] = sib_buf[pl.ds(h * step + ai * aq, aq), :]
     proto_terms(1)
 
     cross = row_buf.at[ITERS + 1]
@@ -352,11 +431,6 @@
                 cross[pos, r : r + 1, :] = across_lanes(total)
     broadcast(CROSS, 2 * ny, pos, at_yc, cross)
 
-    for h in range(2):
-        gathered(EMB_A + h, ny, a_buf.at[h])
-        b_buf[h, bi] = total_of(a_buf.at[h], ny)
-        broadcast(EMB_B + h, ny, bi, at_b, b_buf.at[h])
-
     proto_result(0)
     crossz = rowz_buf.at[ITERS + 1]
     gathered(CROSS, 2 * ny, cross)
@@ -376,8 +450,8 @@
     for h in range(2):
         for d in reversed(far_first(ny)):
             j = lax.rem(ai + d, ny)
-            block = ge_ref.at[pl.ds(c * half + h * step + j * aq, aq)]
-            pltpu.make_async_copy(block, block, ring_sem.at[h, j]).wait()
+            block = ge_ref.at[pl.ds(c * half + (2 * j + h) * aq, aq)]
+            pltpu.make_async_copy(block, block, block_sem.at[h, j]).wait()
             send(TO_SIBLING + h, block, block, sibling)
         sent(TO_SIBLING + h, ge_ref.at[pl.ds(0, step)])
     for h in range(2):
@@ -423,7 +497,10 @@
             pltpu.VMEM((rows, cols), F32),
             pltpu.VMEM((rows, cols), F32),
             pltpu.VMEM((rows, cols), BF16),
-            pltpu.VMEM((rows, width), F32),
+            pltpu.VMEM((ny, 2 * cols, width), BF16),
+            pltpu.VMEM((ny, 2 * aq, 2 * cols), F32),
+            pltpu.VMEM((ny, 2 * aq, 2 * cols), F32),
+            pltpu.VMEM((ny, 2 * aq, 2 * cols), BF16),
             pltpu.VMEM((cols, width), F32),
             pltpu.VMEM((rows, LANES), F32),
             pltpu.VMEM((rows, LANES), F32),
@@ -431,13 +508,13 @@
             pltpu.VMEM((ITERS, nx, SUB, LANES), F32),
             pltpu.VMEM((ITERS + 2, 2 * ny, SUB, LANES), F32),
             pltpu.VMEM((ITERS + 2, ny, SUB, LANES), F32),
-            pltpu.VMEM((samples, width), F32),
-            pltpu.VMEM((2, ny, aq, width), F32),
+            pltpu.VMEM((2 * ny, SUB, LANES), F32),
             pltpu.VMEM((2, ny, aq, width), F32),
             pltpu.VMEM((2, nx, xq, width), F32),
             pltpu.SemaphoreType.DMA((2,)),
             pltpu.SemaphoreType.DMA((STAGES,)),
             pltpu.SemaphoreType.DMA((STAGES,)),
+            pltpu.SemaphoreType.DMA((ny,)),
             pltpu.SemaphoreType.DMA((2, ny)),
         ],
         compiler_params=pltpu.CompilerParams(

time: 95.5 us -> 93 us (0.974)
  Pallas kernels: 94.7 us -> 92.2 us
    pallas_call x1, Pallas kernels: 93.8 us -> 91.3 us  [body(): pl.pallas_call(functools.partial(kernel, nx, ny), out_shape=shapes, in_sp...]
where the time goes in v4:
time: 93 us; the launch traced here: 92.9 us
  Pallas kernels  92.2 us (99%)
    pallas_call x1, Pallas kernels, body(): pl.pallas_call(functools.partial(kernel, nx, ny), out_shape=shapes, in_sp...  91.3 us

profile of v4, /device:TPU:1, one launch (start us, length us, event | category | flops | bytes accessed | tf_op | source)
XLA Modules:
  0.0 92.9 jit_solution(9943893693951642928)
XLA Ops:
  0.6 91.3 %shard_map.49 = (bf16[1024,256]{1,0:T(8,128)(2,1)S(1)}, bf16[512,256]{1,0:T(8,128)(2,1)S(1)}, f32[2,512]{1,0:T(2,128)S(1)}) custom-call(bf16[1024,256]{1,0:T(8,128)(2,1)} %bitcast.2, bf16[512,256]{1,0:T(8,128)(2,1)} %proto_hbm.1), custom_call_target="tpu_custom_call" | custom-call | tf_op jit(solution)/shard_map/pallas_call | solution.py:487
  92.0 0.9 shard_map.50

commit v5 on v4

--- a/solution.py
+++ b/solution.py
@@ -232,6 +232,9 @@
         block = ring_ref.at[slot(offset)]
         pltpu.make_async_copy(block, block, ring_sem.at[slot(offset)]).wait()
 
+    def ring_share():
+        return tcol_ref[pl.ds(pl.multiple_of(c * half + ai * 2 * aq, 2 * aq), 2 * aq), :]
+
     def ring_terms(offset):
         mine = eb_ref[pl.ds(pl.multiple_of(c * half + ai * 2 * aq, 2 * aq), 2 * aq), :]
         other = eb_ref[pl.ds(pl.multiple_of((1 - c) * half + ai * 2 * aq, 2 * aq), 2 * aq), :]
@@ -244,7 +247,10 @@
                 preferred_element_type=F32,
             )
             soft = jnp.exp(s * INV_TEMPER)
-            ring_soft[offset % ny, :, k : k + cols] = soft[: 2 * aq]
+            mine_soft = soft[: 2 * aq]
+            if abs(offset) > 1:
+                mine_soft = mine_soft * jnp.concatenate([ring_share()] * tiles, axis=1)
+            ring_soft[offset % ny, :, k : k + cols] = mine_soft
             ring_sink[offset % ny, :, k : k + cols] = soft[2 * aq :] * soft[2 * aq :]
 
     def row_sums(buf, scale):
@@ -326,6 +332,11 @@
                 send(SCALES, scale_ref, scales_buf.at[z * 2 + c], (x, y * (2 * ny) + lax.rem(z + d, ny) * 2 + 1))
             send(SCALES, scale_ref, scales_buf.at[bi * 2 + c], sibling)
             sent(SCALES, scales_buf.at[pl.ds(0, 2 * ny - 1)])
+            for r in range(SUB):
+                block = slice(r * LANES, (r + 1) * LANES)
+                for j in range(tiles):
+                    k = r // tiles * tiles + j
+                    sink_ref[block, lane[j]] = sink_ref[block, lane[j]] * tens[k : k + 1, :]
         gathered(stage + 1, 2 * ny, row)
         rowz = rowz_buf.at[sweep]
         rowz[z] = total_of(row, 2 * ny)
@@ -334,6 +345,15 @@
             gathered(SOFT + 1, ny, extraz)
             soft_total = total_of(extraz, ny)
             store_columns(tcol_ref, INV_TEMPER / soft_total)
+            for i in range(0, rows, LANES):
+                share = tcol_ref[i : i + LANES, :]
+                for j in range(tiles):
+                    soft_ref[i : i + LANES, lane[j]] = soft_ref[i : i + LANES, lane[j]] * share
+            share = ring_share()
+            for offset in (0, 1, ny - 1):
+                for k in range(2 * tiles):
+                    at = slice(k * LANES, (k + 1) * LANES)
+                    ring_soft[offset, :, at] = ring_soft[offset, :, at] * share
             ring_terms(2)
             ring_terms(-2)
         if sweep == 0:
@@ -344,22 +364,25 @@
             passed(4)
             ring_terms(4)
             gathered(SCALES, 2 * ny, scales_buf)
+            for offset in range(ny):
+                for k in range(2 * tiles):
+                    at = slice(k * LANES, (k + 1) * LANES)
+                    factor = scales_buf[slot(offset) * 2 + k // tiles, pl.ds((1 - c) * tiles + k % tiles, 1), :]
+                    ring_sink[offset, :, at] = ring_sink[offset, :, at] * factor
             flush()
         gathered(stage + 2, ny, rowz)
         weights = 1.0 / total_of(rowz, ny)
         store_columns(wcol_ref, weights)
 
     def slopes(v, h):
-        mine = pl.multiple_of(v * half + h * step, step)
-        other = pl.multiple_of((1 - v) * half + h * step, step)
+        mine = v * half + h * step
+        other = (1 - v) * half + h * step
         for i in range(0, step, LANES):
             here = pl.ds(mine + i, LANES)
             there = pl.ds(other + i, LANES)
             weight = wcol_ref[there, :]
-            share = tcol_ref[here, :]
             for j in range(tiles):
-                pull = sink_ref[there, lane[j]] * scale_ref[pl.ds((1 - v) * tiles + j, 1), :] * weight
-                slope_ref[here, lane[j]] = (soft_ref[here, lane[j]] * share - pull).astype(BF16)
+                slope_ref[here, lane[j]] = (soft_ref[here, lane[j]] - sink_ref[there, lane[j]] * weight).astype(BF16)
 
     def proto_terms(h):
         for k in range(h * xstep, (h + 1) * xstep, LANES):
@@ -392,25 +415,21 @@
         sent(EMB_AG + h, ge_ref.at[pl.ds(0, (ny - 1) * aq)])
         send(TO_SIBLING + h, block, block, sibling)
 
-    share = tcol_ref[pl.ds(pl.multiple_of(c * half + ai * 2 * aq, 2 * aq), 2 * aq), :]
+    for v in range(2):
+        for h in range(2):
+            slopes(v, h)
+    proto_terms(0)
     weight = wcol_ref[pl.ds(pl.multiple_of((1 - c) * half + ai * 2 * aq, 2 * aq), 2 * aq), :]
     total = None
     for offset in range(ny):
         for k in range(2 * tiles):
             at = slice(k * LANES, (k + 1) * LANES)
-            factor = scales_buf[slot(offset) * 2 + k // tiles, pl.ds((1 - c) * tiles + k % tiles, 1), :]
-            pull = ring_sink[offset, :, at] * factor * weight
-            ring_slope[offset, :, at] = (ring_soft[offset, :, at] * share - pull).astype(BF16)
+            ring_slope[offset, :, at] = (ring_soft[offset, :, at] - ring_sink[offset, :, at] * weight).astype(BF16)
         part = jnp.dot(ring_slope[offset], ring_ref[slot(offset)], preferred_element_type=F32)
         total = part if total is None else total + part
     for h in range(2):
         b_buf[h, bi] = total[h * aq : (h + 1) * aq]
         broadcast(EMB_B + h, ny, bi, at_b, b_buf.at[h])
-
-    for v in range(2):
-        for h in range(2):
-            slopes(v, h)
-    proto_terms(0)
     proto_terms(1)
 
     cross = row_buf.at[ITERS + 1]
@@ -424,8 +443,7 @@
                 other = slice((1 - v) * half + i + q, (1 - v) * half + i + q + LANES)
                 total = None
                 for j in range(tiles):
-                    k = (1 - v) * tiles + j
-                    part = sink_ref[other, lane[j]] * scale_ref[k : k + 1, :] * s[q : q + LANES, lane[j]]
+                    part = sink_ref[other, lane[j]] * s[q : q + LANES, lane[j]]
                     total = part if total is None else total + part
                 r = (v * half + i + q) // LANES
                 cross[pos, r : r + 1, :] = across_lanes(total)

time: 93 us -> 91.3 us (0.982)
  Pallas kernels: 92.2 us -> 90.5 us
    pallas_call x1, Pallas kernels: 91.3 us -> 89.6 us  [body(): pl.pallas_call(functools.partial(kernel, nx, ny), out_shape=shapes, in_sp...]
where the time goes in v5:
time: 91.3 us; the launch traced here: 91.2 us
  Pallas kernels  90.5 us (99%)
    pallas_call x1, Pallas kernels, body(): pl.pallas_call(functools.partial(kernel, nx, ny), out_shape=shapes, in_sp...  89.6 us

profile of v5, /device:TPU:1, one launch (start us, length us, event | category | flops | bytes accessed | tf_op | source)
XLA Modules:
  0.0 91.2 jit_solution(4609158853851172675)
XLA Ops:
  0.6 89.6 %shard_map.49 = (bf16[1024,256]{1,0:T(8,128)(2,1)S(1)}, bf16[512,256]{1,0:T(8,128)(2,1)S(1)}, f32[2,512]{1,0:T(2,128)S(1)}) custom-call(bf16[1024,256]{1,0:T(8,128)(2,1)} %bitcast.2, bf16[512,256]{1,0:T(8,128)(2,1)} %proto_hbm.1), custom_call_target="tpu_custom_call" | custom-call | tf_op jit(solution)/shard_map/pallas_call | solution.py:505
  90.3 0.9 shard_map.50

commit v6 on v5

--- a/solution.py
+++ b/solution.py
@@ -455,8 +455,8 @@
     crossz[z] = total_of(cross, 2 * ny)
     broadcast(CROSS + 1, ny, z, at_z, crossz)
     emb_result(0)
+    emb_result(1)
     proto_result(1)
-    emb_result(1)
 
     gathered(CROSS + 1, ny, crossz)
     swapped = jnp.concatenate([weights[tiles:], weights[:tiles]], axis=0)

time: 91.3 us -> 90.1 us (0.987)
  Pallas kernels: 90.5 us -> 89.3 us
    pallas_call x1, Pallas kernels: 89.6 us -> 88.4 us  [body(): pl.pallas_call(functools.partial(kernel, nx, ny), out_shape=shapes, in_sp...]
where the time goes in v6:
time: 90.1 us; the launch traced here: 89.9 us
  Pallas kernels  89.3 us (99%)
    pallas_call x1, Pallas kernels, body(): pl.pallas_call(functools.partial(kernel, nx, ny), out_shape=shapes, in_sp...  88.4 us

profile of v6, /device:TPU:1, one launch (start us, length us, event | category | flops | bytes accessed | tf_op | source)
XLA Modules:
  0.0 89.9 jit_solution(14665645510097800956)
XLA Ops:
  0.6 88.4 %shard_map.49 = (bf16[1024,256]{1,0:T(8,128)(2,1)S(1)}, bf16[512,256]{1,0:T(8,128)(2,1)S(1)}, f32[2,512]{1,0:T(2,128)S(1)}) custom-call(bf16[1024,256]{1,0:T(8,128)(2,1)} %bitcast.2, bf16[512,256]{1,0:T(8,128)(2,1)} %proto_hbm.1), custom_call_target="tpu_custom_call" | custom-call | tf_op jit(solution)/shard_map/pallas_call | solution.py:505
  89.0 0.9 %shard_map.50 = (bf16[1024,256]{1,0:T(8,128)(2,1)}, bf16[512,256]{1,0:T(8,128)(2,1)}, f32[2,512]{1,0:T(2,128)}) custom-call(bf16[1024,256]{1,0:T(8,128)(2,1)S(1)} %get-tuple-element.9.ge_ref, bf16[512,256]{1,0:T(8,128)(2,1)S(1)} %get-tuple-element.10.gp_ref, f32[2,512]{1,0:T(2,128)S(1)} %get-tuple-element.11.loss_ref), custom_call_target="tpu_custom_call" | custom-call | tf_op jit(solution)/shard_map/pallas_call | solution.py:545
